TPU v7x, 256 devices: a whole 4x4x8 slice. The times are simulated.
256 devices in a mesh: example: 64 (over x, z, core), feature: 4 (over y).
Axes of the slice: x: 4, y: 4, z: 8, core: 2. Of those that a mesh axis runs over, the one named last changes fastest.
Arguments:
- embeddings: bfloat16 [36864, 16384], P('example', 'feature'), may hold values from -16 to 16
- subspace: bfloat16 [16384, 128], P('feature'), may hold values from -0.046875 to 0.046875
- noise_levels: int32 [16384, 128], P('feature'), may hold values from -16 to 16
- targets: int32 [2048], replicated, may hold values from 0 to 16383
Outputs:
- embedding_grad: bfloat16 [36864, 16384], P('example', 'feature')
All inputs are finite; a program needn't handle non-finite values.
Results may differ from a plain program's by a relative error of at most 0.0085.
Values may be sent and summed in bfloat16 or wider, within the bound.
A program may use at most 64 MiB of HBM per device.

v0:
```python
import jax
import jax.numpy as jnp
from jax import lax
from jax.sharding import PartitionSpec as P

NOISE_STEP = 1.0 / 4096.0
HIGH = lax.Precision.HIGHEST


def transposed(former, latter, precision=None):
    return lax.dot_general(
        former,
        latter,
        (((0,), (0,)), ((), ())),
        precision=precision,
        preferred_element_type=jnp.float32,
    )


def by_columns(former, latter):
    return lax.dot_general(
        former, latter, (((1,), (1,)), ((), ())), preferred_element_type=jnp.float32
    )


def count_rows(targets, first, length):
    local = targets - first
    inside = (local >= 0) & (local < length)
    slots = jnp.where(inside, local, length)
    ones = jnp.ones(targets.shape, jnp.float32)
    return jax.ops.segment_sum(ones, slots, num_segments=length + 1)[:length]


def upper_factor(gram_matrix):
    return jnp.linalg.cholesky(gram_matrix).T


def factorize(gram_matrix):
    lower_factor = jnp.linalg.cholesky(gram_matrix)
    identity = jnp.eye(gram_matrix.shape[0], dtype=jnp.float32)
    inverse_factor = jax.scipy.linalg.solve_triangular(lower_factor, identity, lower=True)
    gram_inverse = jnp.dot(inverse_factor.T, inverse_factor, precision=HIGH)
    return (inverse_factor, gram_inverse)


def on_device(embeddings, subspace, noise_levels, targets):
    row_count, local_width = embeddings.shape
    examples = lax.axis_size("example")
    total_rows = row_count * examples
    projected = lax.psum(
        jnp.dot(embeddings, subspace, preferred_element_type=jnp.float32), "feature"
    )
    projected_low = projected.astype(jnp.bfloat16)
    feature_first = lax.axis_index("feature") * local_width
    share = local_width // examples
    summed = lax.psum_scatter(
        transposed(embeddings, projected_low), "example", scatter_dimension=0, tiled=True
    )
    offset = lax.axis_index("example") * share
    noise_part = lax.dynamic_slice_in_dim(noise_levels, offset, share, 0)
    image = summed / total_rows + NOISE_STEP * noise_part.astype(jnp.float32)
    row_counts = count_rows(targets, feature_first + offset, share)
    gram_matrix = lax.psum(transposed(image, image, HIGH), ("example", "feature"))
    inverse_factor, gram_inverse = factorize(gram_matrix)
    orthonormal = jnp.dot(image, inverse_factor.T, precision=HIGH)
    alignment = lax.psum(
        transposed(orthonormal * row_counts[:, None], orthonormal, HIGH), ("example", "feature")
    )
    factor_grad = 2.0 * jnp.dot(alignment, inverse_factor, precision=HIGH)
    unused, pull_back = jax.vjp(upper_factor, gram_matrix)
    gram_grad = pull_back(factor_grad)[0]
    image_grad = jnp.dot(image, gram_grad + gram_grad.T, precision=HIGH) - 2.0 * row_counts[
        :, None
    ] * jnp.dot(image, gram_inverse, precision=HIGH)
    grad_low = image_grad.astype(jnp.bfloat16)
    grad_low = lax.all_gather(grad_low, "example", axis=0, tiled=True)
    back_sum = lax.psum(
        jnp.dot(embeddings, grad_low, preferred_element_type=jnp.float32), "feature"
    )
    back_rows = back_sum.astype(jnp.bfloat16)
    result = by_columns(projected_low, grad_low) + by_columns(back_rows, subspace)
    return result.astype(jnp.bfloat16)


def solution(mesh):
    in_specs = (P("example", "feature"), P("feature", None), P("feature", None), P())
    out_specs = P("example", "feature")
    return jax.shard_map(
        on_device, mesh=mesh, in_specs=in_specs, out_specs=out_specs, check_vma=False
    )
```

profile of v0, /device:TPU:2, one launch (start us, length us, event | category | flops | bytes accessed | tf_op | source)
XLA Modules:
  0.0 797.7 jit_solution(3288870860719686440)
XLA Ops:
  6.5 4.2 fusion.45
  10.7 20.2 %all-reduce.8 = bf16[576,128]{1,0:T(8,128)(2,1)S(1)} all-reduce(f32[576,128]{1,0:T(8,128)S(1)} %fusion.45), channel_id=1, replica_groups=mesh['example'=64,'feature'=4] {'feature'}, use_global_device_ids=true, to_apply=%region_0.0 | all-reduce | flops 73728 | bytes 442368 | tf_op jit(solution)/shard_map/psum | solution.py:50
  30.9 4.7 convolution_bitcast_fusion
  35.6 2.9 copy.14
  38.8 14.7 %scatter_custom_fusion = f32[65]{0:T(128)S(1)} fusion(s32[2048]{0:T(1024)S(1)} %and_select_fusion, f32[2048]{0:T(1024)S(1)} %broadcast.95, f32[]{:T(128)} %constant.76.clone.1), kind=kCustom, calls=%fused_computation.59 | custom fusion | flops 2048 | bytes 264 | tf_op jit(solution)/shard_map/scatter-add | solution.py:31
  53.5 126.3 %reduce-scatter.4.cloned.1.call-done = f32[64,128]{1,0:T(8,128)} async-done(((f32[4096,128]{1,0:T(8,128)}), f32[64,128]{1,0:T(8,128)}) %reduce-scatter.4.cloned.1.call-update) | async-done | bytes 32784
  179.7 0.8 copy.15
  180.6 0.9 fusion.46
  181.6 240.4 %all-reduce.5.cloned.1.call-done = f32[128,128]{0,1:T(8,128)} async-done(((f32[128,128]{0,1:T(8,128)}), f32[128,128]{0,1:T(8,128)}) %all-reduce.5.cloned.1.call-update) | async-done | bytes 65552 | tf_op jit(solution)/shard_map/psum | solution.py:63
  422.0 0.9 copy.11
  423.0 0.9 fusion.22
  423.8 11.7 %custom-call.14 = f32[128,128]{1,0:T(8,128)S(1)} custom-call(f32[128,128]{1,0:T(8,128)S(1)} %fusion.22), custom_call_target="Cholesky" | custom-call | tf_op jit(solution)/shard_map/jvp(jit(cholesky))/cholesky/custom-call.1 | solution.py:35
  435.6 0.7 compare_reduce_fusion
  436.9 9.8 %custom-call.13 = f32[1,128,128]{1,2,0:T(8,128)S(1)} custom-call(f32[1,128,128]{2,1,0:T(8,128)S(1)} %fusion.24), custom_call_target="InvertDiagBlocksLowerTriangular" | custom-call | tf_op jit(solution)/shard_map/transpose(jvp(jit(cholesky)))/triangular_solve | solution.py:35
  447.2 1.0 fusion.29
  448.7 233.9 %all-reduce.7.cloned.1.call-done = f32[128,128]{1,0:T(8,128)} async-done(((f32[128,128]{1,0:T(8,128)}), f32[128,128]{1,0:T(8,128)}) %all-reduce.7.cloned.1.call-update) | async-done | bytes 65552 | tf_op jit(solution)/shard_map/psum | solution.py:66
  682.6 1.1 fusion.1
  683.7 0.9 fusion
  685.5 0.9 fusion.3
  686.4 72.9 %all-gather.2.cloned.1.call-done = bf16[4096,128]{1,0:T(8,128)(2,1)} async-done(((bf16[64,128]{1,0:T(8,128)(2,1)}), bf16[4096,128]{1,0:T(8,128)(2,1)}) %all-gather.2.cloned.1.call-update) | async-done | bytes 1048592 | tf_op jit(solution)/shard_map/all_gather | solution.py:76
  759.3 5.2 convolution_bitcast_fusion.1
  764.5 21.6 %all-reduce.9 = bf16[576,128]{0,1:T(8,128)(2,1)S(1)} all-reduce(f32[576,128]{0,1:T(8,128)} %convolution_bitcast_fusion.1), channel_id=1, replica_groups=mesh['example'=64,'feature'=4] {'feature'}, use_global_device_ids=true, to_apply=%region_7.9 | all-reduce | flops 73728 | bytes 442368 | tf_op jit(solution)/shard_map/psum | solution.py:77
  786.1 1.4 fusion.49
  787.5 3.6 add_convert_fusion
  (32 shorter events, 2.9 us)
Async XLA Ops:
  6.5 32.1 %copy-start = (s32[4096,128]{1,0:T(8,128)S(1)}, s32[4096,128]{1,0:T(8,128)}, u32[]{:S(2)}) copy-start(s32[4096,128]{1,0:T(8,128)} %param.7) | copy-start | bytes 6291460
  6.5 173.2 %reduce-scatter.4.cloned.1.call-start = ((), (), s32[]{:S(2)}) async-start(), calls=%async_computation.4 | async-start | bytes 2129920
  35.6 3.2 copy-start.3
  38.6 383.5 %all-reduce.5.cloned.1.call-start = ((), (), s32[]{:S(2)}) async-start(), calls=%async_computation.1 | async-start | bytes 131072 | tf_op jit(solution)/shard_map/psum | solution.py:63
  181.5 501.1 %all-reduce.7.cloned.1.call-start = ((), (), s32[]{:S(2)}) async-start(), calls=%async_computation.2 | async-start | bytes 131072 | tf_op jit(solution)/shard_map/psum | solution.py:66
  448.2 311.1 %all-gather.2.cloned.1.call-start = ((), (), s32[]{:S(2)}) async-start(), calls=%async_computation.3 | async-start | bytes 1064960 | tf_op jit(solution)/shard_map/all_gather | solution.py:76
  759.3 26.8 %copy-start.1 = (bf16[4096,128]{1,0:T(8,128)(2,1)S(1)}, bf16[4096,128]{1,0:T(8,128)(2,1)}, u32[]{:S(2)}) copy-start(bf16[4096,128]{1,0:T(8,128)(2,1)} %all-gather.2.cloned.1.call-done) | copy-start | bytes 3145732
  786.1 1.4 copy-start.2
Sparse Core Ops, SparseCore 0:
  38.7 140.9 reduce-scatter.3
  186.1 235.8 all-reduce.4
  448.3 234.2 all-reduce.6
  686.6 72.6 all-gather.1
where the time goes:
time: 798 us
  waiting for transfers between devices  674 us (84%)
  blocking collectives  41.8 us (5%)
  other arithmetic  38.4 us (5%)
  matrix products  25.4 us (3%)
  between operations  13.3 us (2%)
    psum x1, waiting for transfers between devices, on_device(): lax.psum(transposed(image, image, HIGH), ('example', 'feature'))  240 us
    psum x1, waiting for transfers between devices, on_device(): lax.psum(transposed(orthonormal * row_counts[:, None], orthonormal, HIGH)...  234 us
    unnamed x5, waiting for transfers between devices  126 us
    all_gather x1, waiting for transfers between devices, on_device(): grad_low = lax.all_gather(grad_low, 'example', axis=0, tiled=True)  72.9 us
    another operation x5, other arithmetic, upper_factor(): return jnp.linalg.cholesky(gram_matrix).T  22.8 us
    psum x1, blocking collectives, on_device(): lax.psum(jnp.dot(embeddings, grad_low, preferred_element_type=jnp.float32...  21.6 us
    psum x1, blocking collectives, on_device(): lax.psum(jnp.dot(embeddings, subspace, preferred_element_type=jnp.float32...  20.2 us
  transfers between devices with their start and end apart: 4, of which 4 were waited for; matrix products, arithmetic and copies ran while one was open for 2% of the time, Pallas kernels for 0%

commit v1 on v0

--- a/solution.py
+++ b/solution.py
@@ -73,7 +73,9 @@
         :, None
     ] * jnp.dot(image, gram_inverse, precision=HIGH)
     grad_low = image_grad.astype(jnp.bfloat16)
-    grad_low = lax.all_gather(grad_low, "example", axis=0, tiled=True)
+    grad_low = jnp.concatenate(
+        lax.all_to_all(jnp.stack([grad_low] * lax.axis_size("example")), "example", 0, 0), axis=0
+    )
     back_sum = lax.psum(
         jnp.dot(embeddings, grad_low, preferred_element_type=jnp.float32), "feature"
     )

time: 798 us -> 765 us (0.959)
  waiting for transfers between devices: 674 us -> 601 us
  blocking collectives: 41.8 us -> 75 us
    all_gather x1 -> x0, waiting for transfers between devices: 72.9 us -> none  [on_device(): grad_low = lax.all_gather(grad_low, 'example', axis=0, tiled=True)]
    all_to_all x0 -> x1, blocking collectives: none -> 33.8 us  [on_device(): lax.all_to_all(jnp.stack([grad_low] * lax.axis_size('example')), 'example...]
    unnamed x5 -> x4, waiting for transfers between devices: 126 us -> 126 us
  transfers between devices with their start and end apart: 4 -> 3, of which waited for: 4 -> 3; matrix products, arithmetic and copies ran while one was open for 2% -> 2% of each run, Pallas kernels for 0% -> 0%
where the time goes in v1:
time: 765 us; the launch traced here: 764 us
  waiting for transfers between devices  601 us (79%)
  blocking collectives  75 us (10%)
  other arithmetic  38.4 us (5%)
  matrix products  31.4 us (4%)
  between operations  13.3 us (2%)
    psum x1, waiting for transfers between devices, on_device(): lax.psum(transposed(image, image, HIGH), ('example', 'feature'))  240 us
    psum x1, waiting for transfers between devices, on_device(): lax.psum(transposed(orthonormal * row_counts[:, None], orthonormal, HIGH)...  234 us
    unnamed x4, waiting for transfers between devices  126 us
    all_to_all x1, blocking collectives, on_device(): lax.all_to_all(jnp.stack([grad_low] * lax.axis_size('example')), 'example...  33.8 us
    another operation x5, other arithmetic, upper_factor(): return jnp.linalg.cholesky(gram_matrix).T  22.8 us
    psum x1, blocking collectives, on_device(): lax.psum(jnp.dot(embeddings, grad_low, preferred_element_type=jnp.float32...  21.1 us
    psum x1, blocking collectives, on_device(): lax.psum(jnp.dot(embeddings, subspace, preferred_element_type=jnp.float32...  20.2 us
  transfers between devices with their start and end apart: 3, of which 3 were waited for; matrix products, arithmetic and copies ran while one was open for 2% of the time, Pallas kernels for 0%

profile of v1, /device:TPU:2, one launch (start us, length us, event | category | flops | bytes accessed | tf_op | source)
XLA Modules:
  0.0 764.2 jit_solution(2596139925950020157)
XLA Ops:
  6.5 4.2 fusion.45
  10.7 20.2 %all-reduce.8 = bf16[576,128]{1,0:T(8,128)(2,1)S(1)} all-reduce(f32[576,128]{1,0:T(8,128)S(1)} %fusion.45), channel_id=1, replica_groups=mesh['example'=64,'feature'=4] {'feature'}, use_global_device_ids=true, to_apply=%region_0.0 | all-reduce | flops 73728 | bytes 442368 | tf_op jit(solution)/shard_map/psum | solution.py:50
  30.9 4.7 convolution_bitcast_fusion
  35.6 2.9 copy.14
  38.8 14.7 %scatter_custom_fusion = f32[65]{0:T(128)S(1)} fusion(s32[2048]{0:T(1024)S(1)} %and_select_fusion, f32[2048]{0:T(1024)S(1)} %broadcast.97, f32[]{:T(128)} %constant.76.clone.1), kind=kCustom, calls=%fused_computation.59 | custom fusion | flops 2048 | bytes 264 | tf_op jit(solution)/shard_map/scatter-add | solution.py:31
  53.5 126.3 %reduce-scatter.4.cloned.1.call-done = f32[64,128]{1,0:T(8,128)} async-done(((f32[4096,128]{1,0:T(8,128)}), f32[64,128]{1,0:T(8,128)}) %reduce-scatter.4.cloned.1.call-update) | async-done | bytes 32784
  179.7 0.8 copy.15
  180.6 0.9 fusion.46
  181.8 240.3 %all-reduce.5.cloned.1.call-done = f32[128,128]{0,1:T(8,128)} async-done(((f32[128,128]{0,1:T(8,128)}), f32[128,128]{0,1:T(8,128)}) %all-reduce.5.cloned.1.call-update) | async-done | bytes 65552 | tf_op jit(solution)/shard_map/psum | solution.py:63
  422.0 0.9 copy.11
  423.0 0.9 fusion.22
  423.8 11.7 %custom-call.14 = f32[128,128]{1,0:T(8,128)S(1)} custom-call(f32[128,128]{1,0:T(8,128)S(1)} %fusion.22), custom_call_target="Cholesky" | custom-call | tf_op jit(solution)/shard_map/jvp(jit(cholesky))/cholesky/custom-call.1 | solution.py:35
  435.6 0.7 compare_reduce_fusion
  436.2 0.6 fusion.24
  436.9 9.8 %custom-call.13 = f32[1,128,128]{1,2,0:T(8,128)S(1)} custom-call(f32[1,128,128]{2,1,0:T(8,128)S(1)} %fusion.24), custom_call_target="InvertDiagBlocksLowerTriangular" | custom-call | tf_op jit(solution)/shard_map/transpose(jvp(jit(cholesky)))/triangular_solve | solution.py:35
  447.2 1.0 fusion.29
  448.5 234.1 %all-reduce.7.cloned.1.call-done = f32[128,128]{1,0:T(8,128)} async-done(((f32[128,128]{1,0:T(8,128)}), f32[128,128]{1,0:T(8,128)}) %all-reduce.7.cloned.1.call-update) | async-done | bytes 65552 | tf_op jit(solution)/shard_map/psum | solution.py:66
  682.6 1.1 fusion.1
  683.7 0.9 fusion
  686.1 33.8 %all_to_all.5 = bf16[64,64,128]{2,1,0:T(8,128)(2,1)S(1)} all-to-all(bf16[64,64,128]{2,1,0:T(8,128)(2,1)S(1)} %stack.2), channel_id=1, replica_groups=mesh['example'=64,'feature'=4] {'example'}, dimensions={0} | all-to-all | bytes 2097152 | tf_op jit(solution)/shard_map/all_to_all | solution.py:77
  719.8 4.1 convolution_bitcast_fusion.1
  724.0 5.0 fusion.49
  729.0 21.1 %all-reduce.9 = bf16[576,128]{0,1:T(8,128)(2,1)S(1)} all-reduce(f32[576,128]{0,1:T(8,128)S(1)} %convolution_bitcast_fusion.1), channel_id=1, replica_groups=mesh['example'=64,'feature'=4] {'feature'}, use_global_device_ids=true, to_apply=%region_7.9 | all-reduce | flops 73728 | bytes 442368 | tf_op jit(solution)/shard_map/psum | solution.py:79
  750.1 7.6 add_convert_fusion
  (27 shorter events, 2.7 us)
Async XLA Ops:
  6.5 32.1 %copy-start = (s32[4096,128]{1,0:T(8,128)S(1)}, s32[4096,128]{1,0:T(8,128)}, u32[]{:S(2)}) copy-start(s32[4096,128]{1,0:T(8,128)} %param.7) | copy-start | bytes 6291460
  6.5 173.2 %reduce-scatter.4.cloned.1.call-start = ((), (), s32[]{:S(2)}) async-start(), calls=%async_computation.4 | async-start | bytes 2129920
  35.6 3.2 copy-start.1
  38.6 383.5 %all-reduce.5.cloned.1.call-start = ((), (), s32[]{:S(2)}) async-start(), calls=%async_computation.2 | async-start | bytes 131072 | tf_op jit(solution)/shard_map/psum | solution.py:63
  181.5 501.1 %all-reduce.7.cloned.1.call-start = ((), (), s32[]{:S(2)}) async-start(), calls=%async_computation.3 | async-start | bytes 131072 | tf_op jit(solution)/shard_map/psum | solution.py:66
Sparse Core Ops, SparseCore 0:
  38.7 140.9 reduce-scatter.3
  186.1 235.8 all-reduce.4
  448.3 234.2 all-reduce.6
